TPU v7x, 32 devices: a whole 2x2x4 slice. The times are simulated.
32 devices in a mesh: grp: 2 (over x), din: 16 (over z, y, core).
Axes of the slice: x: 2, y: 2, z: 4, core: 2. Of those that a mesh axis runs over, the one named last changes fastest.
Arguments:
- tokens: bfloat16 [256, 16384], P('grp', 'din'), parts along dimension 0, may hold values from -6 to 6
- norm_gain: bfloat16 [16384], P('din'), may hold values from 0.25 to 1.75
- gate_weight: bfloat16 [16384, 13312], P(None, 'din'), may hold values from -0.046875 to 0.046875
- up_weight: bfloat16 [16384, 13312], P(None, 'din'), may hold values from -0.046875 to 0.046875
- down_weight: bfloat16 [13312, 16384], P('din'), may hold values from -0.078125 to 0.078125
Outputs:
- block_out: bfloat16 [256, 16384], P('grp', 'din'), parts along dimension 0
There are 2 independent parts, one for each index of `grp`. A program takes and returns all parts, laid end to end along the dimension named above; an argument that names none is the same for every part. Nothing has to cross between parts.
All inputs are finite; a program needn't handle non-finite values.
Results may differ from a plain program's by a relative error of at most 0.0066.
Values may be sent and summed in bfloat16 or wider, within the bound.
A program may use at most 256 MiB of HBM per device.

v0:
```python
import jax
import jax.numpy as jnp
from jax import lax
from jax.sharding import PartitionSpec as P


def local(tokens, norm_gain, gate_weight, up_weight, down_weight):
    whole, gain = (
        lax.all_gather(tokens, "din", axis=1, tiled=True),
        lax.all_gather(norm_gain, "din", axis=0, tiled=True),
    )
    values = whole.astype(jnp.float32)
    inverse_rms = lax.rsqrt(jnp.mean(values * values, axis=1, keepdims=True) + 1e-05)
    normed = (values * gain.astype(jnp.float32) * inverse_rms).astype(jnp.bfloat16)
    gate = jnp.dot(normed, gate_weight, preferred_element_type=jnp.float32)
    up = jnp.dot(normed, up_weight, preferred_element_type=jnp.float32)
    hidden = (jax.nn.silu(gate) * up).astype(jnp.bfloat16)
    partial_terms = jnp.dot(hidden, down_weight, preferred_element_type=jnp.float32)
    return lax.psum_scatter(partial_terms, "din", scatter_dimension=1, tiled=True).astype(
        jnp.bfloat16
    )


def solution(mesh):
    in_specs = (P("grp", "din"), P("din"), P(None, "din"), P(None, "din"), P("din", None))
    out_specs = P("grp", "din")
    return jax.shard_map(local, mesh=mesh, in_specs=in_specs, out_specs=out_specs, check_vma=False)
```

profile of v0, /device:TPU:0, one launch (start us, length us, event | category | flops | bytes accessed | tf_op | source)
XLA Modules:
  0.0 223.1 jit_solution(6218927884072042129)
XLA Ops:
  6.5 0.0 all-gather.2.cloned.1.call-start
  6.5 0.7 all-gather.2.cloned.1.call-update
  7.3 0.0 reduce-scatter.2.cloned.1.call-start
  7.3 23.5 %all_gather.7 = bf16[16384]{0:T(1024)(128)(2,1)S(1)} all-gather(bf16[1024]{0:T(1024)(128)(2,1)} %param.6), channel_id=1, replica_groups=mesh['grp'=2,'din'=16] {'din'}, dimensions={0}, use_global_device_ids=true | all-gather | bytes 34816 | tf_op jit(solution)/shard_map/all_gather | solution.py:10
  30.8 32.2 %all-gather.2.cloned.1.call-done = bf16[128,16384]{1,0:T(8,128)(2,1)} async-done(((bf16[128,1024]{1,0:T(8,128)(2,1)}), bf16[128,16384]{1,0:T(8,128)(2,1)}) %all-gather.2.cloned.1.call-update) | async-done | bytes 4194320 | tf_op jit(solution)/shard_map/all_gather | solution.py:9
  63.1 3.1 %fusion.2 = f32[128]{0:T(128)S(1)} fusion(bf16[128,16384]{1,0:T(8,128)(2,1)} %all-gather.2.cloned.1.call-done), kind=kLoop, calls=%fused_computation.4 | loop fusion | flops 6291328 | bytes 4194816 | tf_op jit(solution)/shard_map/reduce_sum | solution.py:13
  66.1 13.7 %fusion.7 = f32[128,832]{0,1:T(8,128)S(1)} fusion(bf16[16384,832]{0,1:T(8,128)(2,1)} %param.7, bf16[128,16384]{1,0:T(8,128)(2,1)} %all-gather.2.cloned.1.call-done, f32[128]{0:T(128)S(1)} %add_rsqrt_fusion, f32[16384]{0:T(1024)S(1)} %convert_element_type.16), kind=kOutput, calls=%fused_computation.8 | convolution fusion | flops 3498049536 | bytes 31949312 | tf_op jit(solution)/shard_map/dot_general | solution.py:15
  79.9 31.1 %fusion.4 = f32[128,16384]{1,0:T(8,128)} fusion(bf16[832,16384]{1,0:T(8,128)(2,1)} %param.9, bf16[16384,832]{0,1:T(8,128)(2,1)} %param.8, bf16[128,16384]{1,0:T(8,128)(2,1)} %all-gather.2.cloned.1.call-done, f32[128]{0:T(128)S(1)} %add_rsqrt_fusion, f32[16384]{0:T(1024)S(1)} %convert_element_type.16, f32[128,832]{0,1:T(8,128)S(1)} %fusion.7), kind=kOutput, calls=%fused_computation.7 | convolution fusion | flops 6988349440 | bytes 67600896 | tf_op jit(solution)/shard_map/dot_general | solution.py:18
  111.0 0.0 reduce-scatter.2.cloned.1.call-update
  111.0 103.5 %reduce-scatter.2.cloned.1.call-done = f32[128,1024]{1,0:T(8,128)} async-done(((f32[128,16384]{1,0:T(8,128)}), f32[128,1024]{1,0:T(8,128)}) %reduce-scatter.2.cloned.1.call-update) | async-done | bytes 524304 | tf_op jit(solution)/shard_map/reduce_scatter | solution.py:19
  214.5 1.8 convert_element_type.19
  (2 shorter events, 0.0 us)
Async XLA Ops:
  6.5 56.5 %all-gather.2.cloned.1.call-start = ((), (), s32[]{:S(2)}) async-start(), calls=%async_computation.1 | async-start | bytes 4456448 | tf_op jit(solution)/shard_map/all_gather | solution.py:9
  7.3 207.2 %reduce-scatter.2.cloned.1.call-start = ((), (), s32[]{:S(2)}) async-start(), calls=%async_computation.2 | async-start | bytes 8912896 | tf_op jit(solution)/shard_map/reduce_scatter | solution.py:19
Sparse Core Ops, SparseCore 0:
  9.5 53.4 all-gather.1
  111.1 103.3 reduce-scatter.1
where the time goes:
time: 223 us
  waiting for transfers between devices  136 us (61%)
  matrix products  44.8 us (20%)
  blocking collectives  23.5 us (11%)
  between operations  13.4 us (6%)
  other arithmetic  4.87 us (2%)
    reduce_scatter x1, waiting for transfers between devices, local(): lax.psum_scatter(partial_terms, 'din', scatter_dimension=1, tiled=True)  103 us
    all_gather x1, waiting for transfers between devices, local(): lax.all_gather(tokens, 'din', axis=1, tiled=True)  32.2 us
    dot_general x1, matrix products, local(): jnp.dot(hidden, down_weight, preferred_element_type=jnp.float32)  31.1 us
    all_gather x1, blocking collectives, local(): lax.all_gather(norm_gain, 'din', axis=0, tiled=True)  23.5 us
    dot_general x1, matrix products, local(): gate = jnp.dot(normed, gate_weight, preferred_element_type=jnp.float32)  13.7 us
  transfers between devices with their start and end apart: 2, of which 2 were waited for; matrix products, arithmetic and copies ran while one was open for 0% of the time, Pallas kernels for 0%

commit v1 on v0

v1 whole, which is shorter than its diff:
```python
import functools

import jax
import jax.numpy as jnp
from jax import lax
from jax.experimental import pallas as pl
from jax.experimental.pallas import tpu as pltpu
from jax.sharding import PartitionSpec as P

NBUF = 4
TILE = 256
EPS = 1e-05


def gathered(tokens, norm_gain, gate_weight, up_weight, down_weight):
    whole, gain = (
        lax.all_gather(tokens, "din", axis=1, tiled=True),
        lax.all_gather(norm_gain, "din", axis=0, tiled=True),
    )
    values = whole.astype(jnp.float32)
    inverse_rms = lax.rsqrt(jnp.mean(values * values, axis=1, keepdims=True) + EPS)
    normed = (values * gain.astype(jnp.float32) * inverse_rms).astype(jnp.bfloat16)
    gate = jnp.dot(normed, gate_weight, preferred_element_type=jnp.float32)
    up = jnp.dot(normed, up_weight, preferred_element_type=jnp.float32)
    hidden = (jax.nn.silu(gate) * up).astype(jnp.bfloat16)
    partial_terms = jnp.dot(hidden, down_weight, preferred_element_type=jnp.float32)
    return lax.psum_scatter(partial_terms, "din", scatter_dimension=1, tiled=True).astype(
        jnp.bfloat16
    )


def ffn_kernel(
    n, x_ref, g_ref, wg_hbm, wu_hbm, wd_hbm, o_ref,
    xbuf, wg, wu, wd, acc_g, acc_u, normed, hid, inv, msg, own, sib_out, sib_in, ring_out, ring_in,
    msg_s, msg_r, ag_s, ag_r, xs_s, xs_r, xo_s, xo_r, w_sem, d_sem, rs_s, rs_r, sb_s, sb_r,
):
    chips = n // 2
    zs = chips // 2
    half = chips // 2
    rows, block = x_ref.shape
    hr = rows // 2
    width = wg_hbm.shape[1]
    features = n * block
    me = lax.axis_index("din")
    core = me % 2
    my_z, my_y = me // 4, (me // 2) % 2
    pos = my_z + my_y * (chips - 1 - 2 * my_z)

    def at(p, c):
        p = (p + 2 * chips) % chips
        y = p // zs
        z = p + y * (chips - 1 - 2 * p)
        return (z * 2 + y) * 2 + c

    other = 1 - core
    sibling = {"din": at(pos, other)}
    toward = ({"din": at(pos + 1, core)}, {"din": at(pos - 1, core)})
    sign = (-1, 1)

    def block_at(j, e):
        k = (j + 1) // 2
        ends = jnp.where(j == 0, 1, jnp.where(j == 2 * half - 1, 1, 0))
        shift = jnp.where(ends == 1, k, (2 * e - 1) * k)
        flip = jnp.where(ends == 1, e, (j + 1) % 2)
        return at(pos + shift, core + flip * (1 - 2 * core))

    def weight_copies(i):
        d = block_at(i // 2, i % 2)
        start = pl.multiple_of(d * block, block)
        b = i % NBUF
        return (
            pltpu.make_async_copy(wg_hbm.at[pl.ds(start, block)], wg.at[b], w_sem.at[0, b]),
            pltpu.make_async_copy(wu_hbm.at[pl.ds(start, block)], wu.at[b], w_sem.at[1, b]),
        )

    def dest_at(t):
        u = t + 2
        k = half - u // 4
        w = u % 4
        mine = jnp.where(k == half, w - 2, jnp.where(k == 0, w % 2, w // 2))
        side = jnp.where(k == half, 1, 1 - 2 * (w % 2))
        c = other + mine * (1 - 2 * other)
        return at(pos + side * k, c)

    def down_copy(t):
        start = pl.multiple_of(dest_at(t) * block, block)
        return pltpu.make_async_copy(wd_hbm.at[:, pl.ds(start, block)], wd.at[t], d_sem.at[t])

    for i in range(NBUF):
        for copy in weight_copies(i):
            copy.start()

    barrier = pltpu.get_barrier_semaphore()

    def greet(k, c):
        pl.semaphore_signal(barrier, inc=1, device_id={"din": (me + k) % n}, device_id_type=pl.DeviceIdType.MESH)
        return c

    lax.fori_loop(1, n, greet, 0)

    xbuf[me] = x_ref[...]
    values = x_ref[...].astype(jnp.float32)
    squares = jnp.sum(values * values, axis=1, keepdims=True)
    msg[me, :, :block] = g_ref[...].astype(jnp.float32)
    msg[me, :, block:] = jnp.transpose(jnp.broadcast_to(squares, (rows, 128)))[0:1, :]
    acc_g[...] = jnp.zeros_like(acc_g)
    acc_u[...] = jnp.zeros_like(acc_u)

    pl.semaphore_wait(barrier, n - 1)

    def msg_copy(k, slot):
        return pltpu.make_async_remote_copy(
            msg.at[slot], msg.at[slot], msg_s.at[k], msg_r.at[k],
            device_id={"din": (me + k) % n}, device_id_type=pl.DeviceIdType.MESH,
        )

    def gather_copy(way, k, h, slot):
        part = xbuf.at[slot, pl.ds(h * hr, hr)]
        return pltpu.make_async_remote_copy(
            part, part, ag_s.at[way, k, h], ag_r.at[way, k, h],
            device_id=toward[way], device_id_type=pl.DeviceIdType.MESH,
        )

    def across_copy(way, k, h, slot):
        part = xbuf.at[slot, pl.ds(h * hr, hr)]
        return pltpu.make_async_remote_copy(
            part, part, xs_s.at[way, k, h], xs_r.at[way, k, h],
            device_id=sibling, device_id_type=pl.DeviceIdType.MESH,
        )

    def own_across(slot):
        return pltpu.make_async_remote_copy(
            xbuf.at[slot], xbuf.at[slot], xo_s, xo_r,
            device_id=sibling, device_id_type=pl.DeviceIdType.MESH,
        )

    def tell(k, c):
        msg_copy(k, me).start()
        return c

    lax.fori_loop(1, n, tell, 0)
    for h in (0, 1):
        for way in (0, 1):
            gather_copy(way, 1, h if way == 0 else 1 - h, me).start()
    own_across(me).start()

    def hear(k, c):
        msg_copy(k, (me - k + n) % n).wait_recv()
        return c

    lax.fori_loop(1, n, hear, 0)
    total = msg[0, :, block:]
    for i in range(1, n):
        total = total + msg[i, :, block:]
    scale = lax.rsqrt(total / features + EPS)
    inv[...] = jnp.transpose(jnp.broadcast_to(scale, (128, rows)))

    def pass_on(k, second):
        for way in (0, 1):
            h = way if not second else 1 - way
            slot = at(pos + sign[way] * k, core)
            gather_copy(way, k, h, slot).wait_recv()

            if second:
                @pl.when(k < half - 1)
                def _():
                    gather_copy(way, k + 1, h, slot).start()
            else:
                @pl.when(k < half)
                def _():
                    gather_copy(way, k + 1, h, slot).start()
            across_copy(way, k, h, slot).start()

    def across_wait(k, second):
        for way in (0, 1):
            h = way if not second else 1 - way
            across_copy(way, k, h, at(pos + sign[way] * k, other)).wait_recv()

    def gate_up(i, c):
        d = block_at(i // 2, i % 2)
        normed[...] = (
            xbuf[d].astype(jnp.float32) * msg[d, :, :block] * inv[:, 0:1]
        ).astype(jnp.bfloat16)
        for copy in weight_copies(i):
            copy.wait()
        b = i % NBUF
        for lo in range(0, width, TILE):
            cols = slice(lo, min(lo + TILE, width))
            acc_g[:, cols] += jnp.dot(normed[...], wg[b, :, cols], preferred_element_type=jnp.float32)
            acc_u[:, cols] += jnp.dot(normed[...], wu[b, :, cols], preferred_element_type=jnp.float32)

        @pl.when(i + NBUF < n)
        def _():
            for copy in weight_copies(i + NBUF):
                copy.start()

        @pl.when(i >= n // 2)
        def _():
            down_copy(2 * (i - n // 2)).start()
            down_copy(2 * (i - n // 2) + 1).start()

        return c

    def pair(j, c):
        @pl.when(j == 0)
        def _():
            own_across(at(pos, other)).wait_recv()

        k = (j + 1) // 2

        @pl.when(j == 1)
        def _():
            pass_on(1, False)

        @pl.when(jnp.logical_and(j % 2 == 1, j < 2 * half - 1))
        def _():
            pass_on(k, True)

        @pl.when(jnp.logical_and(j % 2 == 0, j > 0))
        def _():
            pass_on(k + 1, False)
            across_wait(k, False)
            across_wait(k, True)

        @pl.when(j == 2 * half - 1)
        def _():
            across_wait(half, False)

        return lax.fori_loop(2 * j, 2 * j + 2, gate_up, c)

    lax.fori_loop(0, n // 2, pair, 0)

    for lo in range(0, width, TILE):
        cols = slice(lo, min(lo + TILE, width))
        gate = acc_g[:, cols]
        hid[:, cols] = (gate / (1.0 + jnp.exp(-gate)) * acc_u[:, cols]).astype(jnp.bfloat16)

    def down_tiles(t):
        for lo in range(0, block, TILE):
            cols = slice(lo, lo + TILE)
            yield cols, jnp.dot(hid[...], wd[t, :, cols], preferred_element_type=jnp.float32)

    def sib_copy(p):
        return pltpu.make_async_remote_copy(
            sib_out.at[p], sib_in.at[p], sb_s.at[p], sb_r.at[p],
            device_id=sibling, device_id_type=pl.DeviceIdType.MESH,
        )

    def ring_copy(way, k, h):
        return pltpu.make_async_remote_copy(
            ring_out.at[way, k, pl.ds(h * hr, hr)], ring_in.at[way, k, pl.ds(h * hr, hr)],
            rs_s.at[way, k, h], rs_r.at[way, k, h],
            device_id=toward[way], device_id_type=pl.DeviceIdType.MESH,
        )

    def to_sibling(t, p):
        down_copy(t).wait()
        for cols, tile in down_tiles(t):
            sib_out[p, :, cols] = tile.astype(jnp.bfloat16)
        sib_copy(p).start()

    def to_own(t, side):
        down_copy(t).wait()
        for cols, tile in down_tiles(t):
            own[side, :, cols] = tile

    def ring_send(way, k, h, p, side, chained):
        at_rows = pl.ds(h * hr, hr)
        value = own[side, at_rows, :] + sib_in[p, at_rows, :].astype(jnp.float32)
        if chained:
            ring_copy(way, k + 1, h).wait_recv()
            value = value + ring_in[way, k + 1, at_rows, :].astype(jnp.float32)
        ring_out[way, k, at_rows, :] = value.astype(jnp.bfloat16)
        ring_copy(way, k, h).start()

    to_sibling(0, 0)
    to_own(1, 0)
    sib_copy(0).wait_recv()
    ring_send(0, half, 0, 0, 0, False)
    ring_send(1, half, 1, 0, 0, False)

    def distance(it, c):
        k = half - 1 - it
        t = 2 + 4 * it

        def give(side, c):
            to_sibling(t + side, 1 + 2 * it + side)
            return c

        def keep(side, c):
            to_own(t + 2 + side, side)
            return c

        lax.fori_loop(0, 2, give, 0)
        lax.fori_loop(0, 2, keep, 0)
        for side in (0, 1):
            sib_copy(1 + 2 * it + side).wait_recv()
        for way in (0, 1):
            h = 1 - way

            @pl.when(k == half - 1)
            def _():
                ring_send(way, k, h, 1 + 2 * it + way, way, False)

            @pl.when(k < half - 1)
            def _():
                ring_send(way, k, h, 1 + 2 * it + way, way, True)

        for way in (0, 1):
            ring_send(way, k, way, 1 + 2 * it + way, way, True)
        return c

    lax.fori_loop(0, half - 1, distance, 0)
    last = 2 * half - 1
    to_sibling(n - 2, last)
    to_own(n - 1, 0)
    sib_copy(last).wait_recv()
    own[0] = own[0] + sib_in[last].astype(jnp.float32)
    for h_first in (1, 0):
        for way in (0, 1):
            h = h_first if way == 0 else 1 - h_first
            at_rows = pl.ds(h * hr, hr)
            ring_copy(way, 1, h).wait_recv()
            own[0, at_rows, :] = own[0, at_rows, :] + ring_in[way, 1, at_rows, :].astype(jnp.float32)
    o_ref[...] = own[0].astype(o_ref.dtype)

    def told(k, c):
        msg_copy(k, me).wait_send()
        return c

    lax.fori_loop(1, n, told, 0)
    own_across(me).wait_send()
    for way in (0, 1):
        for k in range(1, half + 1):
            for h in (0, 1):
                if k == half and h != way:
                    continue
                gather_copy(way, k, h, at(pos + sign[way] * (k - 1), core)).wait_send()
                across_copy(way, k, h, at(pos + sign[way] * k, core)).wait_send()
                ring_copy(way, k, h).wait_send()
    for p in range(2 * half):
        sib_copy(p).wait_send()


def ringed(n, tokens, norm_gain, gate_weight, up_weight, down_weight):
    rows, block = tokens.shape
    width = gate_weight.shape[1]
    half = n // 4
    bf16, f32 = jnp.bfloat16, jnp.float32
    dma = pltpu.SemaphoreType.DMA
    vmem = pl.BlockSpec(memory_space=pltpu.VMEM)
    hbm = pl.BlockSpec(memory_space=pl.ANY)
    return pl.pallas_call(
        functools.partial(ffn_kernel, n),
        out_shape=jax.ShapeDtypeStruct((rows, block), bf16),
        in_specs=[vmem, vmem, hbm, hbm, hbm],
        out_specs=vmem,
        scratch_shapes=[
            pltpu.VMEM((n, rows, block), bf16),
            pltpu.VMEM((NBUF, block, width), bf16),
            pltpu.VMEM((NBUF, block, width), bf16),
            pltpu.VMEM((n, width, block), bf16),
            pltpu.VMEM((rows, width), f32),
            pltpu.VMEM((rows, width), f32),
            pltpu.VMEM((rows, block), bf16),
            pltpu.VMEM((rows, width), bf16),
            pltpu.VMEM((rows, 128), f32),
            pltpu.VMEM((n, 1, block + 128), f32),
            pltpu.VMEM((2, rows, block), f32),
            pltpu.VMEM((2 * half, rows, block), bf16),
            pltpu.VMEM((2 * half, rows, block), bf16),
            pltpu.VMEM((2, half + 1, rows, block), bf16),
            pltpu.VMEM((2, half + 1, rows, block), bf16),
            dma((n,)), dma((n,)),
            dma((2, half + 1, 2)), dma((2, half + 1, 2)),
            dma((2, half + 1, 2)), dma((2, half + 1, 2)),
            dma, dma,
            dma((2, NBUF)), dma((n,)),
            dma((2, half + 1, 2)), dma((2, half + 1, 2)),
            dma((2 * half,)), dma((2 * half,)),
        ],
        compiler_params=pltpu.CompilerParams(
            collective_id=0, has_side_effects=True, vmem_limit_bytes=64 * 2**20 - 2**17
        ),
        cost_estimate=pl.CostEstimate(
            flops=6 * rows * n * block * width, bytes_accessed=6 * n * block * width, transcendentals=rows * width
        ),
        name="ffn_ring",
    )(tokens, norm_gain.reshape(1, block), gate_weight, up_weight, down_weight)


def solution(mesh):
    n = mesh.shape["din"]

    def local(tokens, norm_gain, gate_weight, up_weight, down_weight):
        args = (tokens, norm_gain, gate_weight, up_weight, down_weight)
        if n == 16 and tokens.shape[0] == 128 and tokens.shape[1] % TILE == 0 and gate_weight.shape[1] % 16 == 0:
            return ringed(n, *args)
        return gathered(*args)

    in_specs = (P("grp", "din"), P("din"), P(None, "din"), P(None, "din"), P("din", None))
    out_specs = P("grp", "din")
    return jax.shard_map(local, mesh=mesh, in_specs=in_specs, out_specs=out_specs, check_vma=False)
```

time: 223 us -> 139 us (0.62); the launches traced: 223 us -> 137 us
  waiting for transfers between devices: 136 us -> 0 us
  local copies, waits for them, and re-layouts: 0 us -> 76.1 us
  Pallas kernels: 0 us -> 60.5 us
  matrix products: 44.8 us -> 0 us
  blocking collectives: 23.5 us -> 0 us
  between operations: 13.4 us -> 0.01 us
  other arithmetic: 4.87 us -> 0 us
    reduce_scatter x1 -> x0, waiting for transfers between devices: 103 us -> none  [local(): lax.psum_scatter(partial_terms, 'din', scatter_dimension=1, tiled=True)]
    unnamed x0 -> x3, local copies, waits for them, and re-layouts: none -> 74.8 us
    pallas_call x0 -> x1, Pallas kernels: none -> 60.5 us  [ringed(): pl.pallas_call(functools.partial(ffn_kernel, n), out_shape=jax.ShapeDtype...]
    dot_general x2 -> x0, matrix products: 44.8 us -> none  [the longest x1 31.1 us: local(): jnp.dot(hidden, down_weight, preferred_element_type=jnp.float32)]
    all_gather x1 -> x0, waiting for transfers between devices: 32.2 us -> none  [local(): lax.all_gather(tokens, 'din', axis=1, tiled=True)]
    all_gather x1 -> x0, blocking collectives: 23.5 us -> none  [local(): lax.all_gather(norm_gain, 'din', axis=0, tiled=True)]
    reduce_sum x1 -> x0, other arithmetic: 3.08 us -> none  [local(): jnp.mean(values * values, axis=1, keepdims=True) + 1e-05]
  transfers between devices with their start and end apart: 2 -> 0, of which waited for: 2 -> 0; matrix products, arithmetic and copies ran while one was open for 0% -> 0% of each run, Pallas kernels for 0% -> 0%
where the time goes in v1:
time: 139 us; the launch traced here: 137 us
  local copies, waits for them, and re-layouts  76.1 us (55%)
  Pallas kernels  60.5 us (44%)
    unnamed x3, local copies, waits for them, and re-layouts  74.8 us
    pallas_call x1, Pallas kernels, ringed(): pl.pallas_call(functools.partial(ffn_kernel, n), out_shape=jax.ShapeDtype...  60.5 us

profile of v1, /device:TPU:0, one launch (start us, length us, event | category | flops | bytes accessed | tf_op | source)
XLA Modules:
  0.0 136.6 jit_solution(894768534443545266)
XLA Ops:
  0.0 1.3 reshape.3.g_ref
  1.3 36.5 %copy.6.wg_hbm = bf16[16384,832]{1,0:T(8,128)(2,1)} copy(bf16[16384,832]{0,1:T(8,128)(2,1)} %param.7) | data formatting | bytes 54525952 | tf_op args[2]
  37.8 36.6 %copy.7.wu_hbm = bf16[16384,832]{1,0:T(8,128)(2,1)} copy(bf16[16384,832]{0,1:T(8,128)(2,1)} %param.8) | data formatting | bytes 54525952 | tf_op args[3]
  74.4 60.5 %ffn_ring.1 = bf16[128,1024]{1,0:T(8,128)(2,1)} custom-call(bf16[128,1024]{1,0:T(8,128)(2,1)} %x_ref.1, bf16[1,1024]{1,0:T(2,128)(2,1)} %reshape.3.g_ref, bf16[16384,832]{1,0:T(8,128)(2,1)} %copy.6.wg_hbm, bf16[16384,832]{1,0:T(8,128)(2,1)} %copy.7.wu_hbm, bf16[832,16384]{1,0:T(8,128)(2,1)} %wd_hbm.1), custom_call_target="tpu_custom_call" | custom-call | flops 10468982784 | bytes 81788928 | tf_op jit(solution)/shard_map/ffn_ring/pallas_call | solution.py:353
  134.9 1.7 %copy.9 = bf16[128,1024]{1,0:T(8,128)(2,1)} copy(bf16[128,1024]{1,0:T(8,128)(2,1)} %ffn_ring.1) | data formatting | bytes 524288

commit v2 on v1

--- a/solution.py
+++ b/solution.py
@@ -29,6 +29,10 @@
     )
 
 
+def across_last(a, b):
+    return lax.dot_general(a, b, (((1,), (1,)), ((), ())), preferred_element_type=jnp.float32)
+
+
 def ffn_kernel(
     n, x_ref, g_ref, wg_hbm, wu_hbm, wd_hbm, o_ref,
     xbuf, wg, wu, wd, acc_g, acc_u, normed, hid, inv, msg, own, sib_out, sib_in, ring_out, ring_in,
@@ -39,7 +43,7 @@
     half = chips // 2
     rows, block = x_ref.shape
     hr = rows // 2
-    width = wg_hbm.shape[1]
+    width = wg_hbm.shape[0]
     features = n * block
     me = lax.axis_index("din")
     core = me % 2
@@ -69,8 +73,8 @@
         start = pl.multiple_of(d * block, block)
         b = i % NBUF
         return (
-            pltpu.make_async_copy(wg_hbm.at[pl.ds(start, block)], wg.at[b], w_sem.at[0, b]),
-            pltpu.make_async_copy(wu_hbm.at[pl.ds(start, block)], wu.at[b], w_sem.at[1, b]),
+            pltpu.make_async_copy(wg_hbm.at[:, pl.ds(start, block)], wg.at[b], w_sem.at[0, b]),
+            pltpu.make_async_copy(wu_hbm.at[:, pl.ds(start, block)], wu.at[b], w_sem.at[1, b]),
         )
 
     def dest_at(t):
@@ -186,8 +190,8 @@
         b = i % NBUF
         for lo in range(0, width, TILE):
             cols = slice(lo, min(lo + TILE, width))
-            acc_g[:, cols] += jnp.dot(normed[...], wg[b, :, cols], preferred_element_type=jnp.float32)
-            acc_u[:, cols] += jnp.dot(normed[...], wu[b, :, cols], preferred_element_type=jnp.float32)
+            acc_g[:, cols] += across_last(normed[...], wg[b, cols])
+            acc_u[:, cols] += across_last(normed[...], wu[b, cols])
 
         @pl.when(i + NBUF < n)
         def _():
@@ -357,8 +361,8 @@
         out_specs=vmem,
         scratch_shapes=[
             pltpu.VMEM((n, rows, block), bf16),
-            pltpu.VMEM((NBUF, block, width), bf16),
-            pltpu.VMEM((NBUF, block, width), bf16),
+            pltpu.VMEM((NBUF, width, block), bf16),
+            pltpu.VMEM((NBUF, width, block), bf16),
             pltpu.VMEM((n, width, block), bf16),
             pltpu.VMEM((rows, width), f32),
             pltpu.VMEM((rows, width), f32),
@@ -386,7 +390,7 @@
             flops=6 * rows * n * block * width, bytes_accessed=6 * n * block * width, transcendentals=rows * width
         ),
         name="ffn_ring",
-    )(tokens, norm_gain.reshape(1, block), gate_weight, up_weight, down_weight)
+    )(tokens, norm_gain.reshape(1, block), gate_weight.T, up_weight.T, down_weight)
 
 
 def solution(mesh):

time: 139 us -> 66.1 us (0.48); the launches traced: 137 us -> 65.9 us
  local copies, waits for them, and re-layouts: 76.1 us -> 2.95 us
  Pallas kernels: 60.5 us -> 62.9 us
    unnamed x3 -> x1, local copies, waits for them, and re-layouts: 74.8 us -> 1.67 us
    pallas_call x1, Pallas kernels: 60.5 us -> 62.9 us  [ringed(): pl.pallas_call(functools.partial(ffn_kernel, n), out_shape=jax.ShapeDtype...]
where the time goes in v2:
time: 66.1 us; the launch traced here: 65.9 us
  Pallas kernels  62.9 us (95%)
  local copies, waits for them, and re-layouts  2.95 us (4%)
    pallas_call x1, Pallas kernels, ringed(): pl.pallas_call(functools.partial(ffn_kernel, n), out_shape=jax.ShapeDtype...  62.9 us
    unnamed x1, local copies, waits for them, and re-layouts  1.67 us

profile of v2, /device:TPU:0, one launch (start us, length us, event | category | flops | bytes accessed | tf_op | source)
XLA Modules:
  0.0 65.9 jit_solution(9543396861344308772)
XLA Ops:
  0.0 1.3 %reshape.3.g_ref = bf16[1,1024]{1,0:T(2,128)(2,1)} reshape(bf16[1024]{0:T(1024)(128)(2,1)} %param.6) | data formatting | bytes 4096 | tf_op jit(solution)/shard_map/reshape | solution.py:393
  1.3 62.9 %ffn_ring.1 = bf16[128,1024]{1,0:T(8,128)(2,1)} custom-call(bf16[128,1024]{1,0:T(8,128)(2,1)} %x_ref.1, bf16[1,1024]{1,0:T(2,128)(2,1)} %reshape.3.g_ref, bf16[832,16384]{1,0:T(8,128)(2,1)} %bitcast.2, bf16[832,16384]{1,0:T(8,128)(2,1)} %bitcast.3, bf16[832,16384]{1,0:T(8,128)(2,1)} %wd_hbm.1), custom_call_target="tpu_custom_call" | custom-call | flops 10468982784 | bytes 81788928 | tf_op jit(solution)/shard_map/ffn_ring/pallas_call | solution.py:357
  64.2 1.7 %copy.7 = bf16[128,1024]{1,0:T(8,128)(2,1)} copy(bf16[128,1024]{1,0:T(8,128)(2,1)} %ffn_ring.1) | data formatting | bytes 524288

commit v3 on v2

--- a/solution.py
+++ b/solution.py
@@ -8,6 +8,7 @@
 from jax.sharding import PartitionSpec as P
 
 NBUF = 4
+EARLY = 4
 TILE = 256
 EPS = 1e-05
 
@@ -43,6 +44,7 @@
     half = chips // 2
     rows, block = x_ref.shape
     hr = rows // 2
+    hb = block // 2
     width = wg_hbm.shape[0]
     features = n * block
     me = lax.axis_index("din")
@@ -61,21 +63,25 @@
     toward = ({"din": at(pos + 1, core)}, {"din": at(pos - 1, core)})
     sign = (-1, 1)
 
-    def block_at(j, e):
-        k = (j + 1) // 2
-        ends = jnp.where(j == 0, 1, jnp.where(j == 2 * half - 1, 1, 0))
-        shift = jnp.where(ends == 1, k, (2 * e - 1) * k)
-        flip = jnp.where(ends == 1, e, (j + 1) % 2)
-        return at(pos + shift, core + flip * (1 - 2 * core))
-
-    def weight_copies(i):
-        d = block_at(i // 2, i % 2)
-        start = pl.multiple_of(d * block, block)
-        b = i % NBUF
-        return (
-            pltpu.make_async_copy(wg_hbm.at[:, pl.ds(start, block)], wg.at[b], w_sem.at[0, b]),
-            pltpu.make_async_copy(wu_hbm.at[:, pl.ds(start, block)], wu.at[b], w_sem.at[1, b]),
-        )
+    def piece_at(u, e):
+        k = (u + 2) // 4
+        second = ((u + 2) % 4) // 2
+        slot = at(pos + (2 * e - 1) * k, core + (u % 2) * (1 - 2 * core))
+        return slot, e + second * (1 - 2 * e)
+
+    def weight_copies(u):
+        b = u % NBUF
+        copies = []
+        for e in (0, 1):
+            slot, h = piece_at(u, e)
+            source = pl.ds(pl.multiple_of(slot * block + h * hb, hb), hb)
+            for which, (whole, held) in enumerate(((wg_hbm, wg), (wu_hbm, wu))):
+                copies.append(
+                    pltpu.make_async_copy(
+                        whole.at[:, source], held.at[b, :, pl.ds(e * hb, hb)], w_sem.at[which, e, b]
+                    )
+                )
+        return copies
 
     def dest_at(t):
         u = t + 2
@@ -93,6 +99,8 @@
     for i in range(NBUF):
         for copy in weight_copies(i):
             copy.start()
+    for t in range(EARLY):
+        down_copy(t).start()
 
     barrier = pltpu.get_barrier_semaphore()
 
@@ -102,10 +110,11 @@
 
     lax.fori_loop(1, n, greet, 0)
 
-    xbuf[me] = x_ref[...]
+    for h in (0, 1):
+        xbuf[me, h] = x_ref[:, h * hb : (h + 1) * hb]
     values = x_ref[...].astype(jnp.float32)
     squares = jnp.sum(values * values, axis=1, keepdims=True)
-    msg[me, :, :block] = g_ref[...].astype(jnp.float32)
+    msg[me, :, :block] = g_ref[...].astype(jnp.float32).reshape(1, block)
     msg[me, :, block:] = jnp.transpose(jnp.broadcast_to(squares, (rows, 128)))[0:1, :]
     acc_g[...] = jnp.zeros_like(acc_g)
     acc_u[...] = jnp.zeros_like(acc_u)
@@ -119,14 +128,14 @@
         )
 
     def gather_copy(way, k, h, slot):
-        part = xbuf.at[slot, pl.ds(h * hr, hr)]
+        part = xbuf.at[slot, h]
         return pltpu.make_async_remote_copy(
             part, part, ag_s.at[way, k, h], ag_r.at[way, k, h],
             device_id=toward[way], device_id_type=pl.DeviceIdType.MESH,
         )
 
     def across_copy(way, k, h, slot):
-        part = xbuf.at[slot, pl.ds(h * hr, hr)]
+        part = xbuf.at[slot, h]
         return pltpu.make_async_remote_copy(
             part, part, xs_s.at[way, k, h], xs_r.at[way, k, h],
             device_id=sibling, device_id_type=pl.DeviceIdType.MESH,
@@ -142,10 +151,11 @@
         msg_copy(k, me).start()
         return c
 
+    for way in (0, 1):
+        gather_copy(way, 1, way, me).start()
     lax.fori_loop(1, n, tell, 0)
-    for h in (0, 1):
-        for way in (0, 1):
-            gather_copy(way, 1, h if way == 0 else 1 - h, me).start()
+    for way in (0, 1):
+        gather_copy(way, 1, 1 - way, me).start()
     own_across(me).start()
 
     def hear(k, c):
@@ -180,64 +190,56 @@
             h = way if not second else 1 - way
             across_copy(way, k, h, at(pos + sign[way] * k, other)).wait_recv()
 
-    def gate_up(i, c):
-        d = block_at(i // 2, i % 2)
-        normed[...] = (
-            xbuf[d].astype(jnp.float32) * msg[d, :, :block] * inv[:, 0:1]
-        ).astype(jnp.bfloat16)
-        for copy in weight_copies(i):
-            copy.wait()
-        b = i % NBUF
-        for lo in range(0, width, TILE):
-            cols = slice(lo, min(lo + TILE, width))
-            acc_g[:, cols] += across_last(normed[...], wg[b, cols])
-            acc_u[:, cols] += across_last(normed[...], wu[b, cols])
-
-        @pl.when(i + NBUF < n)
-        def _():
-            for copy in weight_copies(i + NBUF):
-                copy.start()
-
-        @pl.when(i >= n // 2)
-        def _():
-            down_copy(2 * (i - n // 2)).start()
-            down_copy(2 * (i - n // 2) + 1).start()
-
-        return c
-
-    def pair(j, c):
-        @pl.when(j == 0)
+    def unit(u, c):
+        k = (u + 2) // 4
+        second = ((u + 2) % 4) // 2
+        mine = u % 2 == 0
+
+        @pl.when(u == 1)
         def _():
             own_across(at(pos, other)).wait_recv()
 
-        k = (j + 1) // 2
-
-        @pl.when(j == 1)
+        for turn in (0, 1):
+            now = jnp.logical_and(u > 1, second == turn)
+
+            @pl.when(jnp.logical_and(now, mine))
+            def _():
+                pass_on(k, turn == 1)
+
+            @pl.when(jnp.logical_and(now, u % 2 == 1))
+            def _():
+                across_wait(k, turn == 1)
+
+        for e in (0, 1):
+            slot, h = piece_at(u, e)
+            gain = msg[slot, :, pl.ds(pl.multiple_of(h * hb, hb), hb)]
+            normed[:, e * hb : (e + 1) * hb] = (
+                xbuf[slot, h].astype(jnp.float32) * gain * inv[:, 0:1]
+            ).astype(jnp.bfloat16)
+        for copy in weight_copies(u):
+            copy.wait()
+        b = u % NBUF
+        acc_g[...] += across_last(wg[b], normed[...])
+        acc_u[...] += across_last(wu[b], normed[...])
+
+        @pl.when(u + NBUF < n)
         def _():
-            pass_on(1, False)
-
-        @pl.when(jnp.logical_and(j % 2 == 1, j < 2 * half - 1))
+            for copy in weight_copies(u + NBUF):
+                copy.start()
+
+        @pl.when(u + EARLY < n)
         def _():
-            pass_on(k, True)
-
-        @pl.when(jnp.logical_and(j % 2 == 0, j > 0))
-        def _():
-            pass_on(k + 1, False)
-            across_wait(k, False)
-            across_wait(k, True)
-
-        @pl.when(j == 2 * half - 1)
-        def _():
-            across_wait(half, False)
-
-        return lax.fori_loop(2 * j, 2 * j + 2, gate_up, c)
-
-    lax.fori_loop(0, n // 2, pair, 0)
-
-    for lo in range(0, width, TILE):
-        cols = slice(lo, min(lo + TILE, width))
-        gate = acc_g[:, cols]
-        hid[:, cols] = (gate / (1.0 + jnp.exp(-gate)) * acc_u[:, cols]).astype(jnp.bfloat16)
+            down_copy(u + EARLY).start()
+
+        return c
+
+    lax.fori_loop(0, n, unit, 0)
+
+    for lo in range(0, width, 128):
+        part = slice(lo, min(lo + 128, width))
+        gate = acc_g[part]
+        hidden = gate / (1.0 + jnp.exp(-gate)) * acc_u[part]
+        hid[:, part] = jnp.transpose(hidden).astype(jnp.bfloat16)
 
     def down_tiles(t):
         for lo in range(0, block, TILE):
@@ -360,12 +362,12 @@
         in_specs=[vmem, vmem, hbm, hbm, hbm],
         out_specs=vmem,
         scratch_shapes=[
-            pltpu.VMEM((n, rows, block), bf16),
+            pltpu.VMEM((n, 2, rows, block // 2), bf16),
             pltpu.VMEM((NBUF, width, block), bf16),
             pltpu.VMEM((NBUF, width, block), bf16),
             pltpu.VMEM((n, width, block), bf16),
-            pltpu.VMEM((rows, width), f32),
-            pltpu.VMEM((rows, width), f32),
+            pltpu.VMEM((width, rows), f32),
+            pltpu.VMEM((width, rows), f32),
             pltpu.VMEM((rows, block), bf16),
             pltpu.VMEM((rows, width), bf16),
             pltpu.VMEM((rows, 128), f32),
@@ -379,7 +381,7 @@
             dma((2, half + 1, 2)), dma((2, half + 1, 2)),
             dma((2, half + 1, 2)), dma((2, half + 1, 2)),
             dma, dma,
-            dma((2, NBUF)), dma((n,)),
+            dma((2, 2, NBUF)), dma((n,)),
             dma((2, half + 1, 2)), dma((2, half + 1, 2)),
             dma((2 * half,)), dma((2 * half,)),
         ],
@@ -390,7 +392,7 @@
             flops=6 * rows * n * block * width, bytes_accessed=6 * n * block * width, transcendentals=rows * width
         ),
         name="ffn_ring",
-    )(tokens, norm_gain.reshape(1, block), gate_weight.T, up_weight.T, down_weight)
+    )(tokens, norm_gain, gate_weight.T, up_weight.T, down_weight)
 
 
 def solution(mesh):

time: 66.1 us -> 62.9 us (0.952)
  Pallas kernels: 62.9 us -> 61.1 us
  local copies, waits for them, and re-layouts: 2.95 us -> 1.67 us
    pallas_call x1, Pallas kernels: 62.9 us -> 61.1 us  [ringed(): pl.pallas_call(functools.partial(ffn_kernel, n), out_shape=jax.ShapeDtype...]
    reshape x1 -> x0, local copies, waits for them, and re-layouts: 1.28 us -> none  [ringed(): norm_gain.reshape(1, block)]
where the time goes in v3:
time: 62.9 us; the launch traced here: 62.8 us
  Pallas kernels  61.1 us (97%)
  local copies, waits for them, and re-layouts  1.67 us (3%)
    pallas_call x1, Pallas kernels, ringed(): pl.pallas_call(functools.partial(ffn_kernel, n), out_shape=jax.ShapeDtype...  61.1 us
    unnamed x1, local copies, waits for them, and re-layouts  1.67 us

profile of v3, /device:TPU:0, one launch (start us, length us, event | category | flops | bytes accessed | tf_op | source)
XLA Modules:
  0.0 62.8 jit_solution(7971311372466378505)
XLA Ops:
  0.0 61.1 %ffn_ring.1 = bf16[128,1024]{1,0:T(8,128)(2,1)} custom-call(bf16[128,1024]{1,0:T(8,128)(2,1)} %x_ref.1, bf16[1024]{0:T(1024)(128)(2,1)} %g_ref.1, bf16[832,16384]{1,0:T(8,128)(2,1)} %bitcast.2, bf16[832,16384]{1,0:T(8,128)(2,1)} %bitcast.3, bf16[832,16384]{1,0:T(8,128)(2,1)} %wd_hbm.1), custom_call_target="tpu_custom_call" | custom-call | flops 10468982784 | bytes 81788928 | tf_op jit(solution)/shard_map/ffn_ring/pallas_call | solution.py:359
  61.1 1.7 %copy.7 = bf16[128,1024]{1,0:T(8,128)(2,1)} copy(bf16[128,1024]{1,0:T(8,128)(2,1)} %ffn_ring.1) | data formatting | bytes 524288

commit v4 on v3

--- a/solution.py
+++ b/solution.py
@@ -193,20 +193,19 @@
     def unit(u, c):
         k = (u + 2) // 4
         second = ((u + 2) % 4) // 2
-        mine = u % 2 == 0
+        piece = jnp.where(u == n - 2, n // 2 - 1, jnp.where(u > n - 4, 0, (u + 1) // 2))
+        due = jnp.where(u == n - 2, 1, u % 2) * jnp.minimum(piece, 1)
 
         @pl.when(u == 1)
         def _():
             own_across(at(pos, other)).wait_recv()
 
         for turn in (0, 1):
-            now = jnp.logical_and(u > 1, second == turn)
-
-            @pl.when(jnp.logical_and(now, mine))
+            @pl.when(jnp.logical_and(due == 1, (piece + 1) % 2 == turn))
             def _():
-                pass_on(k, turn == 1)
-
-            @pl.when(jnp.logical_and(now, u % 2 == 1))
+                pass_on((piece + 1) // 2, turn == 1)
+
+            @pl.when(jnp.logical_and(jnp.logical_and(u > 1, second == turn), u % 2 == 1))
             def _():
                 across_wait(k, turn == 1)
 

time: 62.9 us -> 63.2 us (level)
  no operation moved by 1% of the time
where the time goes in v4:
time: 63.2 us; the launch traced here: 63 us
  Pallas kernels  61.3 us (97%)
  local copies, waits for them, and re-layouts  1.67 us (3%)
    pallas_call x1, Pallas kernels, ringed(): pl.pallas_call(functools.partial(ffn_kernel, n), out_shape=jax.ShapeDtype...  61.3 us
    unnamed x1, local copies, waits for them, and re-layouts  1.67 us

profile of v4, /device:TPU:0, one launch (start us, length us, event | category | flops | bytes accessed | tf_op | source)
XLA Modules:
  0.0 63.0 jit_solution(17840618522576466574)
XLA Ops:
  0.0 61.3 %ffn_ring.1 = bf16[128,1024]{1,0:T(8,128)(2,1)} custom-call(bf16[128,1024]{1,0:T(8,128)(2,1)} %x_ref.1, bf16[1024]{0:T(1024)(128)(2,1)} %g_ref.1, bf16[832,16384]{1,0:T(8,128)(2,1)} %bitcast.2, bf16[832,16384]{1,0:T(8,128)(2,1)} %bitcast.3, bf16[832,16384]{1,0:T(8,128)(2,1)} %wd_hbm.1), custom_call_target="tpu_custom_call" | custom-call | flops 10468982784 | bytes 81788928 | tf_op jit(solution)/shard_map/ffn_ring/pallas_call | solution.py:358
  61.4 1.7 %copy.7 = bf16[128,1024]{1,0:T(8,128)(2,1)} copy(bf16[128,1024]{1,0:T(8,128)(2,1)} %ffn_ring.1) | data formatting | bytes 524288
